TPU v7x, 256 devices: a whole 4x4x8 slice. The times are simulated.
256 devices in a mesh: dp: 4 (over x), node: 8 (over y, core), local: 8 (over z).
Axes of the slice: x: 4, y: 4, z: 8, core: 2. Of those that a mesh axis runs over, the one named last changes fastest.
Arguments:
- tokens: bfloat16 [4096, 3584], P(('dp', 'node', 'local')), may hold values from -6 to 6
- cotangent: bfloat16 [4096, 3584], P(('dp', 'node', 'local')), may hold values from -6 to 6
- routes: int32 [4096, 8], P(('dp', 'node', 'local')), may hold values from 0 to 63, as said below
- gates: bfloat16 [4096, 8], P(('dp', 'node', 'local')), may hold values from 0.099609375 to 0.5
- w_gate: bfloat16 [64, 3584, 1024], P(('node', 'local'), None, 'dp'), may hold values from -0.09375 to 0.09375
- w_up: bfloat16 [64, 3584, 1024], P(('node', 'local'), None, 'dp'), may hold values from -0.09375 to 0.09375
- w_down: bfloat16 [64, 1024, 3584], P(('node', 'local'), 'dp'), may hold values from -0.1875 to 0.1875
Outputs:
- d_tokens: bfloat16 [4096, 3584], P(('dp', 'node', 'local'))
- d_gates: float32 [4096, 8], P(('dp', 'node', 'local'))
- grad_gate: bfloat16 [64, 3584, 1024], P(('node', 'local'), None, 'dp')
- grad_up: bfloat16 [64, 3584, 1024], P(('node', 'local'), None, 'dp')
- grad_down: bfloat16 [64, 1024, 3584], P(('node', 'local'), 'dp')
Inputs may be any that keep to these rules, and one draw needn't show every extreme that they name: `routes`: each row names 8 different experts, 2 in each of exactly 4 node groups, expert e lying in node group e // 8. Among the rows of one device each node group is named by exactly 8 rows and no expert by more than 3 rows; in every draw each node group has an expert named by exactly 3 rows of every device.
All inputs are finite; a program needn't handle non-finite values.
Results may differ from a plain program's by a relative error of at most 0.0075.
Values may be sent and summed in bfloat16 or wider, within the bound.
No kernel may reach another device: no remote copies, remote signals or barrier semaphores. Data moves between devices by JAX's collectives and lax.ppermute only.
A program may use at most 128 MiB of HBM per device.

v0:
```python
import jax
import jax.numpy as jnp
from jax import lax
from jax.experimental import pallas as pl
from jax.experimental.pallas import tpu as pltpu
from jax.sharding import PartitionSpec as P

F32 = jnp.float32
BF16 = jnp.bfloat16
GROUP_MAX = 4
LANES = 128
CHUNK = 1792


def shift(value, step):
    size = lax.axis_size("dp")
    return lax.ppermute(value, "dp", [(i, (i + step) % size) for i in range(size)])


def swap(value):
    return lax.all_to_all(value, ("node", "local"), split_axis=0, concat_axis=0, tiled=True)


def by_device(value, peers):
    return value.reshape(peers, -1, LANES)


def dot(a, b, ca, cb):
    return lax.dot_general(a, b, (((ca,), (cb,)), ((), ())), preferred_element_type=F32)


def expert_kernel(steps, count, *refs):
    x_refs, dy_refs, refs = refs[:count], refs[count:2 * count], refs[2 * count:]
    gate_ref, up_ref, down_ref, d_gate_ref, d_up_ref, hidden_ref = refs[:6]
    out_refs, (gate_acc, up_acc, d_hidden_acc) = refs[6:-3], refs[-3:]

    def put(value, begin):
        first = 0
        for ref in out_refs:
            last = first + ref.shape[0]
            ref[:, pl.ds(begin, value.shape[1])] = value[first:last]
            first = last
    phase, step = pl.program_id(0), pl.program_id(1)

    @pl.when(phase == 0)
    def _():
        @pl.when(step == 0)
        def _():
            gate_acc[...] = jnp.zeros_like(gate_acc)
            up_acc[...] = jnp.zeros_like(up_acc)
            d_hidden_acc[...] = jnp.zeros_like(d_hidden_acc)

        rows_x = jnp.concatenate([ref[...] for ref in x_refs], axis=0)
        rows_dy = jnp.concatenate([ref[...] for ref in dy_refs], axis=0)
        gate_acc[...] += dot(rows_x, gate_ref[...], 1, 0)
        up_acc[...] += dot(rows_x, up_ref[...], 1, 0)
        d_hidden_acc[...] += dot(rows_dy, down_ref[...], 1, 1)

        @pl.when(step == steps - 1)
        def _():
            gate_pre, up_pre, d_hidden = gate_acc[...], up_acc[...], d_hidden_acc[...]
            sigmoid_gate = jax.nn.sigmoid(gate_pre)
            activated = gate_pre * sigmoid_gate
            hidden = (activated * up_pre).astype(BF16)
            hidden_ref[...] = hidden
            d_gate_ref[...] = (
                d_hidden * up_pre * sigmoid_gate * (1.0 + gate_pre * (1.0 - sigmoid_gate))
            ).astype(BF16)
            d_up_ref[...] = (d_hidden * activated).astype(BF16)
            gate_rows = jnp.sum(hidden.astype(F32) * d_hidden, axis=1, keepdims=True)
            high = gate_rows.astype(BF16).astype(F32)
            lane = lax.broadcasted_iota(jnp.int32, (gate_rows.shape[0], LANES), 1)
            extra = jnp.where(lane == 0, high, jnp.where(lane == 1, gate_rows - high, 0.0))
            put(extra.astype(BF16), steps * CHUNK)

    @pl.when(phase == 1)
    def _():
        value = dot(d_gate_ref[...], gate_ref[...], 1, 1) + dot(d_up_ref[...], up_ref[...], 1, 1)
        put(value.astype(BF16), pl.multiple_of(step * CHUNK, CHUNK))


def expert_rows(blocks, sizes, gate_mat, up_mat, down_mat):
    width, hidden_width = gate_mat.shape
    steps = width // CHUNK
    rows = sum(block.shape[0] for block in blocks)
    small = jax.ShapeDtypeStruct((rows, hidden_width), BF16)
    whole = pl.BlockSpec((rows, hidden_width), lambda p, k: (0, 0))

    def part(block, first):
        return pl.BlockSpec(
            (block.shape[0], CHUNK), lambda p, k: (0, first + k * (1 - p) + (steps - 1) * p)
        )

    return pl.pallas_call(
        lambda *refs: expert_kernel(steps, len(blocks), *refs),
        grid=(2, steps),
        in_specs=[part(block, 0) for block in blocks]
        + [part(block, steps) for block in blocks]
        + [
            pl.BlockSpec((CHUNK, hidden_width), lambda p, k: (k, 0)),
            pl.BlockSpec((CHUNK, hidden_width), lambda p, k: (k, 0)),
            pl.BlockSpec((hidden_width, CHUNK), lambda p, k: (0, k * (1 - p) + (steps - 1) * p)),
        ],
        out_specs=[whole] * 3
        + [pl.BlockSpec((size, width + LANES), lambda p, k: (0, 0)) for size in sizes],
        out_shape=[small] * 3
        + [jax.ShapeDtypeStruct((size, width + LANES), BF16) for size in sizes],
        scratch_shapes=[pltpu.VMEM((rows, hidden_width), F32)] * 3,
        compiler_params=pltpu.CompilerParams(vmem_limit_bytes=60 * 1024 * 1024),
        cost_estimate=pl.CostEstimate(flops=1000000, bytes_accessed=1000000, transcendentals=0),
    )(*blocks, *blocks, gate_mat, up_mat, down_mat)


def local(tokens, cotangent, routes, gates, w_gate, w_up, w_down):
    tok_dev, width = tokens.shape
    top = routes.shape[1]
    nodes = lax.axis_size("node")
    experts = nodes * lax.axis_size("local")
    group_rows = tok_dev * min(GROUP_MAX, nodes) // nodes
    most = min(group_rows, max(2, tok_dev * top // experts + 1))

    named = routes[:, :, None] == jnp.arange(experts, dtype=jnp.int32)
    member = jnp.any(named, axis=1)
    member_i = member.astype(jnp.int32)
    rank = jnp.cumsum(member_i, axis=0) - member_i
    rank = jnp.where(member, rank, most).astype(BF16)
    weight = jnp.sum(jnp.where(named, gates.astype(F32)[:, :, None], 0.0), axis=1)

    def seat_table(first, count):
        columns = experts * count
        spread = lax.broadcasted_iota(jnp.int32, (experts, columns), 1) // count
        spread = (spread == lax.broadcasted_iota(jnp.int32, (experts, columns), 0)).astype(BF16)
        seat_of = lax.broadcasted_iota(jnp.int32, (tok_dev, columns), 1) % count + first
        seats = dot(rank, spread, 1, 0).astype(jnp.int32) == seat_of
        return seats, jnp.where(seats, dot(weight.astype(BF16), spread, 1, 0), 0.0).astype(BF16)

    tables = [seat_table(0, 1), seat_table(1, most - 1)]
    both = jnp.concatenate([tokens, cotangent], axis=1)

    down_mat = w_down[0]
    hidden_width = down_mat.shape[0]
    bar = lax.optimization_barrier

    def pick(turn):
        return by_device(dot(tables[turn][0].astype(BF16), both, 0, 0).astype(BF16), experts)

    def flat(raw, columns):
        return raw.reshape(-1, columns)

    def ring_one(own):
        return shift(own, -1), shift(own, 1)

    def ring_two(up, down):
        size = up.shape[0] // 2
        return shift(up[:size], -1), shift(down[size:], 1)

    def forward(blocks, sizes):
        d_gate_pre, d_up_pre, hidden, *parts = expert_rows(blocks, sizes, w_gate[0], w_up[0], down_mat)
        return (blocks, d_gate_pre, d_up_pre, hidden), parts

    def merge(first, second):
        return (first.astype(F32) + second.astype(F32)).astype(BF16)

    def grads(saved, sums):
        blocks, d_gate_pre, d_up_pre, hidden = saved
        rows_x = jnp.concatenate([block[:, :width] for block in blocks], axis=0)
        rows_dy = jnp.concatenate([block[:, width:] for block in blocks], axis=0)
        return (
            sums[0] + dot(rows_x, d_gate_pre, 0, 0),
            sums[1] + dot(rows_x, d_up_pre, 0, 0),
            sums[2] + dot(hidden, rows_dy, 0, 0),
        )

    raw0 = swap(pick(0))
    send1, raw0 = bar((pick(1), raw0))
    own0 = flat(raw0, 2 * width)
    one0 = ring_one(own0)
    raw1 = swap(send1)
    two0 = ring_two(*one0)
    own0, one0, two0, raw1 = bar((own0, one0, two0, raw1))
    own1 = flat(raw1, 2 * width)
    one1 = ring_one(own1)
    size = own0.shape[0] // 2
    group0, parts0 = forward(two0 + one0 + (own0,), [size] * 6 + [2 * size])
    far_top, far_low, up_top, up_low, down_top, down_low, mine0 = parts0
    relays0 = shift(far_top, 1), shift(far_low, -1)
    own1, one1, relays0, up_top, up_low, down_top, down_low, mine0 = bar(
        (own1, one1, relays0, up_top, up_low, down_top, down_low, mine0)
    )
    up0 = jnp.concatenate([merge(up_top, relays0[0]), up_low], axis=0)
    down0 = jnp.concatenate([down_top, merge(down_low, relays0[1])], axis=0)
    up0, down0, own1, one1 = bar((up0, down0, own1, one1))
    two1 = ring_two(*one1)
    came0 = shift(up0, 1), shift(down0, -1)
    size = own1.shape[0] // 2
    near1, parts1 = forward(one1 + (own1,), [size] * 4 + [2 * size])
    two1, came0, parts1 = bar((two1, came0, parts1))
    up_top, up_low, down_top, down_low, mine = parts1
    early = shift(up_low, 1), shift(down_top, -1)
    far1, far = forward(two1, [size] * 2)
    relays = shift(far[0], 1), shift(far[1], -1)
    came0, _ = bar((came0, far))
    total0 = merge(mine0.astype(F32) + came0[0].astype(F32), came0[1])
    send_home0 = by_device(total0, experts)
    home0 = swap(send_home0)
    came_top = shift(merge(up_top, relays[0]), 1)
    came_low = shift(merge(down_low, relays[1]), -1)
    came_up = jnp.concatenate([came_top, early[0]], axis=0).astype(F32)
    came_down = jnp.concatenate([early[1], came_low], axis=0)
    group0, _ = bar((group0, send_home0))
    sums = grads(group0, (0.0, 0.0, 0.0))
    total1, home0, sums = bar((merge(mine.astype(F32) + came_up, came_down), home0, sums))
    send_home1 = by_device(total1, experts)
    home1 = swap(send_home1)

    d_tokens, d_weight = 0.0, 0.0
    for (seats, combine), home in zip(tables, (home0, home1)):
        home = home.reshape(seats.shape[1], width + LANES)
        d_tokens = d_tokens + dot(combine, home[:, :width], 1, 0)
        extra = home[:, width:].astype(F32)
        d_seat = jnp.where(seats, (extra[:, 0] + extra[:, 1])[None, :], 0.0)
        d_weight = d_weight + jnp.sum(d_seat.reshape(tok_dev, experts, -1), axis=2)
    d_tokens = d_tokens.astype(BF16)
    d_gates = jnp.sum(jnp.where(named, d_weight[:, None, :], 0.0), axis=2)

    near1, far1, _ = bar((near1, far1, send_home1))
    grad_gate, grad_up, grad_down = grads(far1, grads(near1, sums))
    grad_gate, grad_up, grad_down = [
        value.astype(BF16)[None] for value in (grad_gate, grad_up, grad_down)
    ]
    return d_tokens, d_gates, grad_gate, grad_up, grad_down


def solution(mesh):
    rows = P(("dp", "node", "local"), None)
    wide = P(("node", "local"), None, "dp")
    tall = P(("node", "local"), "dp", None)
    return jax.shard_map(
        local,
        mesh=mesh,
        in_specs=(rows, rows, rows, rows, wide, wide, tall),
        out_specs=(rows, rows, wide, wide, tall),
        check_vma=False,
    )
```

profile of v0, /device:TPU:1, one launch (start us, length us, event | category | flops | bytes accessed | tf_op | source)
XLA Modules:
  0.0 276.1 jit_solution(5487882420570288187)
XLA Ops:
  5.0 13.2 %all-to-all-start = ((bf16[64,56,128]{2,1,0:T(8,128)(2,1)}), bf16[64,56,128]{2,1,0:T(8,128)(2,1)S(1)}, u32[]{:S(2)}, u32[]{:S(2)}) async-start(bf16[64,56,128]{2,1,0:T(8,128)(2,1)} %bitcast.8), calls=%async_computation | async-start | bytes 1835008 | tf_op jit(solution)/shard_map/all_to_all | solution.py:21
  19.1 1.8 reshape.66
  20.9 22.7 %all-to-all-done = bf16[64,56,128]{2,1,0:T(8,128)(2,1)S(1)} async-done(((bf16[64,56,128]{2,1,0:T(8,128)(2,1)}), bf16[64,56,128]{2,1,0:T(8,128)(2,1)S(1)}, u32[]{:S(2)}, u32[]{:S(2)}) %all-to-all-start) | async-done | bytes 917536 | tf_op jit(solution)/shard_map/all_to_all | solution.py:21
  43.5 7.0 %all-to-all-start.1 = ((bf16[64,112,128]{2,1,0:T(8,128)(2,1)}), bf16[64,112,128]{2,1,0:T(8,128)(2,1)}, u32[]{:S(2)}, u32[]{:S(2)}) async-start(bf16[64,112,128]{2,1,0:T(8,128)(2,1)} %reshape.66), calls=%async_computation.1 | async-start | bytes 3670016 | tf_op jit(solution)/shard_map/all_to_all | solution.py:21
  54.6 20.0 %collective-permute-done.1.refs_3_.refs_8_ = bf16[64,7168]{1,0:T(8,128)(2,1)S(1)} collective-permute-done((bf16[64,7168]{1,0:T(8,128)(2,1)S(1)}, bf16[64,7168]{1,0:T(8,128)(2,1)S(1)}, u32[]{:S(2)}, u32[]{:S(2)}) %collective-permute-start.1) | collective-permute-done | bytes 917536 | tf_op jit(solution)/shard_map/ppermute | solution.py:17
  76.5 1.9 collective-permute-start.2
  78.3 8.5 %collective-permute-done.3.refs_1_.refs_6_ = bf16[32,7168]{1,0:T(8,128)(2,1)S(1)} collective-permute-done((bf16[32,7168]{1,0:T(8,128)(2,1)S(1)}, bf16[32,7168]{1,0:T(8,128)(2,1)S(1)}, u32[]{:S(2)}, u32[]{:S(2)}) %collective-permute-start.3) | collective-permute-done | bytes 458784 | tf_op jit(solution)/shard_map/ppermute | solution.py:17
  87.3 9.2 %all-to-all-done.1 = bf16[64,112,128]{2,1,0:T(8,128)(2,1)} async-done(((bf16[64,112,128]{2,1,0:T(8,128)(2,1)}), bf16[64,112,128]{2,1,0:T(8,128)(2,1)}, u32[]{:S(2)}, u32[]{:S(2)}) %all-to-all-start.1) | async-done | bytes 1835040 | tf_op jit(solution)/shard_map/all_to_all | solution.py:21
  96.5 2.7 reshape.69.refs_2_.refs_5_
  102.0 8.5 %shard_map.110 = (bf16[256,256]{1,0:T(8,128)(2,1)}, bf16[256,256]{1,0:T(8,128)(2,1)}, bf16[256,256]{1,0:T(8,128)(2,1)}, bf16[32,3712]{1,0:T(8,128)(2,1)}, bf16[3...) custom-call(bf16[32,7168]{1,0:T(8,128)(2,1)} %collective-permute-don, ...), custom_call_target="tpu_custom_call" | custom-call | flops 1000000 | bytes 1000000 | tf_op jit(solution)/shard_map/pallas_call | solution.py:94
  110.7 2.7 collective-permute-start.7
  113.3 33.5 %collective-permute-done.6 = bf16[32,3712]{1,0:T(8,128)(2,1)S(1)} collective-permute-done((bf16[32,3712]{1,0:T(8,128)(2,1)}, bf16[32,3712]{1,0:T(8,128)(2,1)S(1)}, u32[]{:S(2)}, u32[]{:S(2)}) %collective-permute-start.6) | collective-permute-done | bytes 237600 | tf_op jit(solution)/shard_map/ppermute | solution.py:17
  152.2 2.2 slice.99
  157.1 2.7 collective-permute-start.11
  159.9 9.9 %shard_map.111 = (bf16[384,256]{1,0:T(8,128)(2,1)}, bf16[384,256]{1,0:T(8,128)(2,1)}, bf16[384,256]{1,0:T(8,128)(2,1)}, bf16[64,3712]{1,0:T(8,128)(2,1)}, bf16[6...) custom-call(bf16[128,7168]{1,0:T(8,128)(2,1)} %collective-permute-done.4.re, ...), custom_call_target="tpu_custom_call" | custom-call | flops 1000000 | bytes 1000000 | tf_op jit(solution)/shard_map/pallas_call | solution.py:94
  169.8 17.9 %collective-permute-done.10 = bf16[64,3712]{1,0:T(8,128)(2,1)} collective-permute-done((bf16[64,3712]{1,0:T(8,128)(2,1)S(1)}, bf16[64,3712]{1,0:T(8,128)(2,1)}, u32[]{:S(2)}, u32[]{:S(2)}) %collective-permute-start.10) | collective-permute-done | bytes 475168 | tf_op jit(solution)/shard_map/ppermute | solution.py:17
  188.2 2.3 collective-permute-start.15
  190.5 7.4 %shard_map.112 = (bf16[128,256]{1,0:T(8,128)(2,1)}, bf16[128,256]{1,0:T(8,128)(2,1)}, bf16[128,256]{1,0:T(8,128)(2,1)}, bf16[64,3712]{1,0:T(8,128)(2,1)}, bf16[64,3712]{1,0:T(8,128)(2,1)}) custom-call(bf16[64,7168]{1,0:T(8,128)(2,1)} %copy-done.13, bf16[64,7168]{1,0:T(8,128)(2,1)} %copy-done.11, bf16[64,7168]{1,0:T(8,128)(2,1)} %copy-done.13, ...), custom_call_target="tpu_custom_call" | custom-call | flops 1000000 | bytes 1000000 | tf_op jit(solution)/shard_map/pallas_call | solution.py:94
  197.9 2.7 collective-permute-start.16
  203.0 7.8 %all-to-all-start.2 = ((bf16[64,29,128]{2,1,0:T(8,128)(2,1)}), bf16[64,29,128]{2,1,0:T(8,128)(2,1)S(1)}, u32[]{:S(2)}, u32[]{:S(2)}) async-start(bf16[64,29,128]{2,1,0:T(8,128)(2,1)} %reshape.70), calls=%async_computation.2 | async-start | bytes 1048576 | tf_op jit(solution)/shard_map/all_to_all | solution.py:21
  213.4 2.5 fusion.57
  216.3 2.7 collective-permute-start.17
  219.0 2.5 fusion.56
  221.5 2.6 fusion.58
  224.0 5.0 %collective-permute-done.13 = bf16[64,3712]{1,0:T(8,128)(2,1)S(1)} collective-permute-done((bf16[64,3712]{1,0:T(8,128)(2,1)S(1)}, bf16[64,3712]{1,0:T(8,128)(2,1)S(1)}, u32[]{:S(2)}, u32[]{:S(2)}) %collective-permute-start.13) | collective-permute-done | bytes 475168 | tf_op jit(solution)/shard_map/ppermute | solution.py:17
  230.7 2.2 reshape.72
  232.9 11.5 %all-to-all-start.3 = ((bf16[64,58,128]{2,1,0:T(8,128)(2,1)}), bf16[64,58,128]{2,1,0:T(8,128)(2,1)S(1)}, u32[]{:S(2)}, u32[]{:S(2)}) async-start(bf16[64,58,128]{2,1,0:T(8,128)(2,1)} %reshape.72), calls=%async_computation.3 | async-start | bytes 2097152 | tf_op jit(solution)/shard_map/all_to_all | solution.py:21
  248.7 1.9 copy-done.4
  252.1 1.9 fusion.3
  256.3 1.9 fusion.5
  260.4 1.9 fusion.4
  262.3 10.2 %all-to-all-done.3 = bf16[64,58,128]{2,1,0:T(8,128)(2,1)S(1)} async-done(((bf16[64,58,128]{2,1,0:T(8,128)(2,1)}), bf16[64,58,128]{2,1,0:T(8,128)(2,1)S(1)}, u32[]{:S(2)}, u32[]{:S(2)}) %all-to-all-start.3) | async-done | bytes 950304 | tf_op jit(solution)/shard_map/all_to_all | solution.py:21
  (147 shorter events, 43.7 us)
Async XLA Ops:
  5.0 38.5 %all-to-all-start = ((bf16[64,56,128]{2,1,0:T(8,128)(2,1)}), bf16[64,56,128]{2,1,0:T(8,128)(2,1)S(1)}, u32[]{:S(2)}, u32[]{:S(2)}) async-start(bf16[64,56,128]{2,1,0:T(8,128)(2,1)} %bitcast.8), calls=%async_computation | async-start | bytes 1835008 | tf_op jit(solution)/shard_map/all_to_all | solution.py:21
  43.5 7.0 %copy-start.17 = (bf16[64,56,128]{2,1,0:T(8,128)(2,1)}, bf16[64,56,128]{2,1,0:T(8,128)(2,1)S(1)}, u32[]{:S(2)}) copy-start(bf16[64,56,128]{2,1,0:T(8,128)(2,1)S(1)} %all-to-all-done) | copy-start | bytes 2752516
  43.5 53.0 %all-to-all-start.1 = ((bf16[64,112,128]{2,1,0:T(8,128)(2,1)}), bf16[64,112,128]{2,1,0:T(8,128)(2,1)}, u32[]{:S(2)}, u32[]{:S(2)}) async-start(bf16[64,112,128]{2,1,0:T(8,128)(2,1)} %reshape.66), calls=%async_computation.1 | async-start | bytes 3670016 | tf_op jit(solution)/shard_map/all_to_all | solution.py:21
  51.8 47.4 %copy-start.2 = (bf16[8,8,56,128]{3,1,2,0:T(8,128)(2,1)}, bf16[8,8,56,128]{3,1,2,0:T(8,128)(2,1)S(1)}, u32[]{:S(2)}) copy-start(bf16[8,8,56,128]{3,1,2,0:T(8,128)(2,1)S(1)} %copy.39) | copy-start | bytes 2752516
  51.8 22.8 %collective-permute-start.1 = (bf16[64,7168]{1,0:T(8,128)(2,1)S(1)}, bf16[64,7168]{1,0:T(8,128)(2,1)S(1)}, u32[]{:S(2)}, u32[]{:S(2)}) collective-permute-start(bf16[64,7168]{1,0:T(8,128)(2,1)S(1)} %bitcast.48), channel_id=1, source_target_pairs={{0,64},{64,128},{128,192},{192,0},{1,65},{65,129},{129,193},{193,1... | collective-permute-start | bytes 2752520 | tf_op jit(solution)/shard_map/ppermute | solution.py:17
  53.1 21.6 %collective-permute-start = (bf16[64,7168]{1,0:T(8,128)(2,1)S(1)}, bf16[64,7168]{1,0:T(8,128)(2,1)S(1)}, u32[]{:S(2)}, u32[]{:S(2)}) collective-permute-start(bf16[64,7168]{1,0:T(8,128)(2,1)S(1)} %bitcast.49), channel_id=1, source_target_pairs={{0,192},{64,0},{128,64},{192,128},{1,193},{65,1},{129,65},{193,129... | collective-permute-start | bytes 2752520 | tf_op jit(solution)/shard_map/ppermute | solution.py:17
  74.6 12.1 %collective-permute-start.3 = (bf16[32,7168]{1,0:T(8,128)(2,1)S(1)}, bf16[32,7168]{1,0:T(8,128)(2,1)S(1)}, u32[]{:S(2)}, u32[]{:S(2)}) collective-permute-start(bf16[32,7168]{1,0:T(8,128)(2,1)S(1)} %slice.129), channel_id=1, source_target_pairs={{0,64},{64,128},{128,192},{192,0},{1,65},{65,129},{129,193},{193,1... | collective-permute-start | bytes 1376264 | tf_op jit(solution)/shard_map/ppermute | solution.py:17
  76.5 10.9 %collective-permute-start.2 = (bf16[32,7168]{1,0:T(8,128)(2,1)S(1)}, bf16[32,7168]{1,0:T(8,128)(2,1)}, u32[]{:S(2)}, u32[]{:S(2)}) collective-permute-start(bf16[32,7168]{1,0:T(8,128)(2,1)S(1)} %slice.128), channel_id=1, source_target_pairs={{0,192},{64,0},{128,64},{192,128},{1,193},{65,1},{129,65},{193,129... | collective-permute-start | bytes 1376264 | tf_op jit(solution)/shard_map/ppermute | solution.py:17
  86.8 15.2 %copy-start.15 = (bf16[32,7168]{1,0:T(8,128)(2,1)}, bf16[32,7168]{1,0:T(8,128)(2,1)S(1)}, u32[]{:S(2)}) copy-start(bf16[32,7168]{1,0:T(8,128)(2,1)S(1)} %collective-permute-done.3.refs_1_.refs_6_) | copy-start | bytes 1376260
  99.3 11.3 %copy-start = (bf16[128,7168]{1,0:T(8,128)(2,1)}, bf16[128,7168]{1,0:T(8,128)(2,1)S(1)}, u32[]{:S(2)}) copy-start(bf16[128,7168]{1,0:T(8,128)(2,1)S(1)} %reshape.69.refs_2_.refs_5_) | copy-start | bytes 5505028
  99.3 47.9 %collective-permute-start.5 = (bf16[128,7168]{1,0:T(8,128)(2,1)S(1)}, bf16[128,7168]{1,0:T(8,128)(2,1)}, u32[]{:S(2)}, u32[]{:S(2)}) collective-permute-start(bf16[128,7168]{1,0:T(8,128)(2,1)S(1)} %reshape.69.refs_2_.refs_5_), channel_id=1, source_target_pairs={{0,64},{64,128},{128,192},{192,0},{1,65},{65,129},{129,193},{193,1... | collective-permute-start | bytes 5505032 | tf_op jit(solution)/shard_map/ppermute | solution.py:17
  100.6 46.6 %collective-permute-start.4 = (bf16[128,7168]{1,0:T(8,128)(2,1)S(1)}, bf16[128,7168]{1,0:T(8,128)(2,1)}, u32[]{:S(2)}, u32[]{:S(2)}) collective-permute-start(bf16[128,7168]{1,0:T(8,128)(2,1)S(1)} %reshape.69.refs_2_.refs_5_), channel_id=1, source_target_pairs={{0,192},{64,0},{128,64},{192,128},{1,193},{65,1},{129,65},{193,129... | collective-permute-start | bytes 5505032 | tf_op jit(solution)/shard_map/ppermute | solution.py:17
  110.6 39.6 %copy-start.22 = (bf16[32,3712]{1,0:T(8,128)(2,1)S(1)}, bf16[32,3712]{1,0:T(8,128)(2,1)}, u32[]{:S(2)}) copy-start(bf16[32,3712]{1,0:T(8,128)(2,1)} %get-tuple-element.104) | copy-start | bytes 712708
  110.6 36.3 %collective-permute-start.6 = (bf16[32,3712]{1,0:T(8,128)(2,1)}, bf16[32,3712]{1,0:T(8,128)(2,1)S(1)}, u32[]{:S(2)}, u32[]{:S(2)}) collective-permute-start(bf16[32,3712]{1,0:T(8,128)(2,1)} %get-tuple-element.94), channel_id=1, source_target_pairs={{0,64},{64,128},{128,192},{192,0},{1,65},{65,129},{129,193},{193,1... | collective-permute-start | bytes 712712 | tf_op jit(solution)/shard_map/ppermute | solution.py:17
  110.7 36.5 %collective-permute-start.7 = (bf16[32,3712]{1,0:T(8,128)(2,1)}, bf16[32,3712]{1,0:T(8,128)(2,1)S(1)}, u32[]{:S(2)}, u32[]{:S(2)}) collective-permute-start(bf16[32,3712]{1,0:T(8,128)(2,1)} %get-tuple-element.95), channel_id=1, source_target_pairs={{0,192},{64,0},{128,64},{192,128},{1,193},{65,1},{129,65},{193,129... | collective-permute-start | bytes 712712 | tf_op jit(solution)/shard_map/ppermute | solution.py:17
  151.0 8.8 %copy-start.30 = (bf16[16,8]{0,1:T(8,128)(2,1)S(1)}, bf16[16,8]{0,1:T(8,128)(2,1)}, u32[]{:S(2)}) copy-start(bf16[16,8]{0,1:T(8,128)(2,1)} %param.10) | copy-start | bytes 772
  154.4 33.3 %collective-permute-start.9 = (bf16[64,7168]{1,0:T(8,128)(2,1)}, bf16[64,7168]{1,0:T(8,128)(2,1)S(1)}, u32[]{:S(2)}, u32[]{:S(2)}) collective-permute-start(bf16[64,7168]{1,0:T(8,128)(2,1)} %slice.99), channel_id=1, source_target_pairs={{0,64},{64,128},{128,192},{192,0},{1,65},{65,129},{129,193},{193,1... | collective-permute-start | bytes 2752520 | tf_op jit(solution)/shard_map/ppermute | solution.py:17
  155.6 32.1 %collective-permute-start.8 = (bf16[64,7168]{1,0:T(8,128)(2,1)S(1)}, bf16[64,7168]{1,0:T(8,128)(2,1)S(1)}, u32[]{:S(2)}, u32[]{:S(2)}) collective-permute-start(bf16[64,7168]{1,0:T(8,128)(2,1)S(1)} %slice.98), channel_id=1, source_target_pairs={{0,192},{64,0},{128,64},{192,128},{1,193},{65,1},{129,65},{193,129... | collective-permute-start | bytes 2752520 | tf_op jit(solution)/shard_map/ppermute | solution.py:17
  157.1 30.6 %collective-permute-start.10 = (bf16[64,3712]{1,0:T(8,128)(2,1)S(1)}, bf16[64,3712]{1,0:T(8,128)(2,1)}, u32[]{:S(2)}, u32[]{:S(2)}) collective-permute-start(bf16[64,3712]{1,0:T(8,128)(2,1)S(1)} %pad_maximum_fusion.6), channel_id=1, source_target_pairs={{0,64},{64,128},{128,192},{192,0},{1,65},{65,129},{129,193},{193,1... | collective-permute-start | bytes 1425416 | tf_op jit(solution)/shard_map/ppermute | solution.py:17
  157.1 30.6 %collective-permute-start.11 = (bf16[64,3712]{1,0:T(8,128)(2,1)}, bf16[64,3712]{1,0:T(8,128)(2,1)}, u32[]{:S(2)}, u32[]{:S(2)}) collective-permute-start(bf16[64,3712]{1,0:T(8,128)(2,1)} %pad_maximum_fusion.7), channel_id=1, source_target_pairs={{0,192},{64,0},{128,64},{192,128},{1,193},{65,1},{129,65},{193,129... | collective-permute-start | bytes 1425416 | tf_op jit(solution)/shard_map/ppermute | solution.py:17
  187.7 12.8 %copy-start.21 = (bf16[64,3712]{1,0:T(8,128)(2,1)S(1)}, bf16[64,3712]{1,0:T(8,128)(2,1)}, u32[]{:S(2)}) copy-start(bf16[64,3712]{1,0:T(8,128)(2,1)} %get-tuple-element.129) | copy-start | bytes 1425412
  187.7 36.3 %collective-permute-start.14 = (bf16[64,3712]{1,0:T(8,128)(2,1)}, bf16[64,3712]{1,0:T(8,128)(2,1)S(1)}, u32[]{:S(2)}, u32[]{:S(2)}) collective-permute-start(bf16[64,3712]{1,0:T(8,128)(2,1)} %get-tuple-element.125), channel_id=1, source_target_pairs={{0,64},{64,128},{128,192},{192,0},{1,65},{65,129},{129,193},{193,1... | collective-permute-start | bytes 1425416 | tf_op jit(solution)/shard_map/ppermute | solution.py:17
  188.2 35.9 %collective-permute-start.15 = (bf16[64,3712]{1,0:T(8,128)(2,1)}, bf16[64,3712]{1,0:T(8,128)(2,1)}, u32[]{:S(2)}, u32[]{:S(2)}) collective-permute-start(bf16[64,3712]{1,0:T(8,128)(2,1)} %get-tuple-element.126), channel_id=1, source_target_pairs={{0,192},{64,0},{128,64},{192,128},{1,193},{65,1},{129,65},{193,129... | collective-permute-start | bytes 1425416 | tf_op jit(solution)/shard_map/ppermute | solution.py:17
  197.9 18.0 %collective-permute-start.12 = (bf16[64,3712]{1,0:T(8,128)(2,1)}, bf16[64,3712]{1,0:T(8,128)(2,1)S(1)}, u32[]{:S(2)}, u32[]{:S(2)}) collective-permute-start(bf16[64,3712]{1,0:T(8,128)(2,1)} %get-tuple-element.124), channel_id=1, source_target_pairs={{0,64},{64,128},{128,192},{192,0},{1,65},{65,129},{129,193},{193,1... | collective-permute-start | bytes 1425416 | tf_op jit(solution)/shard_map/ppermute | solution.py:17
  197.9 18.2 %collective-permute-start.16 = (bf16[64,3712]{1,0:T(8,128)(2,1)}, bf16[64,3712]{1,0:T(8,128)(2,1)S(1)}, u32[]{:S(2)}, u32[]{:S(2)}) collective-permute-start(bf16[64,3712]{1,0:T(8,128)(2,1)} %get-tuple-element.128), channel_id=1, source_target_pairs={{0,192},{64,0},{128,64},{192,128},{1,193},{65,1},{129,65},{193,129... | collective-permute-start | bytes 1425416 | tf_op jit(solution)/shard_map/ppermute | solution.py:17
  201.9 10.1 %copy-start.16 = (bf16[32,7168]{1,0:T(8,128)(2,1)S(1)}, bf16[32,7168]{1,0:T(8,128)(2,1)}, u32[]{:S(2)}) copy-start(bf16[32,7168]{1,0:T(8,128)(2,1)} %copy-done.15) | copy-start | bytes 1376260
  201.9 10.2 %copy-start.8 = (bf16[64,7168]{1,0:T(8,128)(2,1)S(1)}, bf16[64,7168]{1,0:T(8,128)(2,1)}, u32[]{:S(2)}) copy-start(bf16[64,7168]{1,0:T(8,128)(2,1)} %copy-done.7) | copy-start | bytes 2752516
  203.0 27.4 %all-to-all-start.2 = ((bf16[64,29,128]{2,1,0:T(8,128)(2,1)}), bf16[64,29,128]{2,1,0:T(8,128)(2,1)S(1)}, u32[]{:S(2)}, u32[]{:S(2)}) async-start(bf16[64,29,128]{2,1,0:T(8,128)(2,1)} %reshape.70), calls=%async_computation.2 | async-start | bytes 1048576 | tf_op jit(solution)/shard_map/all_to_all | solution.py:21
  216.0 13.0 %collective-permute-start.13 = (bf16[64,3712]{1,0:T(8,128)(2,1)S(1)}, bf16[64,3712]{1,0:T(8,128)(2,1)S(1)}, u32[]{:S(2)}, u32[]{:S(2)}) collective-permute-start(bf16[64,3712]{1,0:T(8,128)(2,1)S(1)} %add_convert_fusion.3), channel_id=1, source_target_pairs={{0,64},{64,128},{128,192},{192,0},{1,65},{65,129},{129,193},{193,1... | collective-permute-start | bytes 1425416 | tf_op jit(solution)/shard_map/ppermute | solution.py:17
  216.3 12.8 %collective-permute-start.17 = (bf16[64,3712]{1,0:T(8,128)(2,1)S(1)}, bf16[64,3712]{1,0:T(8,128)(2,1)S(1)}, u32[]{:S(2)}, u32[]{:S(2)}) collective-permute-start(bf16[64,3712]{1,0:T(8,128)(2,1)S(1)} %add_convert_fusion.2), channel_id=1, source_target_pairs={{0,192},{64,0},{128,64},{192,128},{1,193},{65,1},{129,65},{193,129... | collective-permute-start | bytes 1425416 | tf_op jit(solution)/shard_map/ppermute | solution.py:17
  221.5 7.6 %copy-start.18 = (bf16[128,3712]{1,0:T(8,128)(2,1)S(1)}, bf16[128,3712]{1,0:T(8,128)(2,1)}, u32[]{:S(2)}) copy-start(bf16[128,3712]{1,0:T(8,128)(2,1)} %get-tuple-element.120) | copy-start | bytes 2850820
  232.9 39.6 %all-to-all-start.3 = ((bf16[64,58,128]{2,1,0:T(8,128)(2,1)}), bf16[64,58,128]{2,1,0:T(8,128)(2,1)S(1)}, u32[]{:S(2)}, u32[]{:S(2)}) async-start(bf16[64,58,128]{2,1,0:T(8,128)(2,1)} %reshape.72), calls=%async_computation.3 | async-start | bytes 2097152 | tf_op jit(solution)/shard_map/all_to_all | solution.py:21
  (23 other events, 49.9 us)
where the time goes:
time: 277 us; the launch traced here: 276 us
  waiting for transfers between devices  128 us (46%)
  starting transfers between devices  63.2 us (23%)
  local copies, waits for them, and re-layouts  30.3 us (11%)
  Pallas kernels  25.8 us (9%)
  matrix products  20.1 us (7%)
  other arithmetic  7.6 us (3%)
    ppermute x18, waiting for transfers between devices, shift(): lax.ppermute(value, 'dp', [(i, (i + step) % size) for i in range(size)])  85.7 us
    all_to_all x4, waiting for transfers between devices, swap(): lax.all_to_all(value, ('node', 'local'), split_axis=0, concat_axis=0, til...  42.1 us
    all_to_all x4, starting transfers between devices, swap(): lax.all_to_all(value, ('node', 'local'), split_axis=0, concat_axis=0, til...  39.5 us
    pallas_call x3, Pallas kernels, expert_rows(): pl.pallas_call(lambda *refs: expert_kernel(steps, len(blocks), *refs), gr...  25.8 us
    ppermute x18, starting transfers between devices, shift(): lax.ppermute(value, 'dp', [(i, (i + step) % size) for i in range(size)])  23.8 us
    dot_general x15, matrix products, dot(): lax.dot_general(a, b, (((ca,), (cb,)), ((), ())), preferred_element_type=...  20.1 us
    unnamed x76, local copies, waits for them, and re-layouts  13.1 us
  transfers between devices with their start and end apart: 22, of which 10 were waited for; matrix products, arithmetic and copies ran while one was open for 11% of the time, Pallas kernels for 9%

commit v1 on v0

--- a/solution.py
+++ b/solution.py
@@ -184,13 +184,13 @@
     group0, parts0 = forward(two0 + one0 + (own0,), [size] * 6 + [2 * size])
     far_top, far_low, up_top, up_low, down_top, down_low, mine0 = parts0
     relays0 = shift(far_top, 1), shift(far_low, -1)
-    own1, one1, relays0, up_top, up_low, down_top, down_low, mine0 = bar(
-        (own1, one1, relays0, up_top, up_low, down_top, down_low, mine0)
+    own1, one1, up_top, up_low, down_top, down_low, mine0 = bar(
+        (own1, one1, up_top, up_low, down_top, down_low, mine0)
     )
+    two1 = ring_two(*one1)
     up0 = jnp.concatenate([merge(up_top, relays0[0]), up_low], axis=0)
     down0 = jnp.concatenate([down_top, merge(down_low, relays0[1])], axis=0)
     up0, down0, own1, one1 = bar((up0, down0, own1, one1))
-    two1 = ring_two(*one1)
     came0 = shift(up0, 1), shift(down0, -1)
     size = own1.shape[0] // 2
     near1, parts1 = forward(one1 + (own1,), [size] * 4 + [2 * size])

time: 277 us -> 269 us (0.971)
  waiting for transfers between devices: 128 us -> 124 us
  other arithmetic: 7.6 us -> 4.78 us
    ppermute x18, waiting for transfers between devices: 85.7 us -> 80.9 us  [shift(): lax.ppermute(value, 'dp', [(i, (i + step) % size) for i in range(size)])]
    unnamed x76 -> x80, local copies, waits for them, and re-layouts: 13.1 us -> 11.9 us
  transfers between devices with their start and end apart: 22 -> 22, of which waited for: 10 -> 10; matrix products, arithmetic and copies ran while one was open for 11% -> 13% of each run, Pallas kernels for 9% -> 10%
where the time goes in v1:
time: 269 us; the launch traced here: 268 us
  waiting for transfers between devices  124 us (46%)
  starting transfers between devices  62.2 us (23%)
  local copies, waits for them, and re-layouts  29.2 us (11%)
  Pallas kernels  25.8 us (10%)
  matrix products  20.1 us (7%)
  other arithmetic  4.78 us (2%)
    ppermute x18, waiting for transfers between devices, shift(): lax.ppermute(value, 'dp', [(i, (i + step) % size) for i in range(size)])  80.9 us
    all_to_all x4, waiting for transfers between devices, swap(): lax.all_to_all(value, ('node', 'local'), split_axis=0, concat_axis=0, til...  43.3 us
    all_to_all x4, starting transfers between devices, swap(): lax.all_to_all(value, ('node', 'local'), split_axis=0, concat_axis=0, til...  38.2 us
    pallas_call x3, Pallas kernels, expert_rows(): pl.pallas_call(lambda *refs: expert_kernel(steps, len(blocks), *refs), gr...  25.8 us
    ppermute x18, starting transfers between devices, shift(): lax.ppermute(value, 'dp', [(i, (i + step) % size) for i in range(size)])  24 us
    dot_general x15, matrix products, dot(): lax.dot_general(a, b, (((ca,), (cb,)), ((), ())), preferred_element_type=...  20.1 us
    unnamed x80, local copies, waits for them, and re-layouts  11.9 us
  transfers between devices with their start and end apart: 22, of which 10 were waited for; matrix products, arithmetic and copies ran while one was open for 13% of the time, Pallas kernels for 10%

profile of v1, /device:TPU:1, one launch (start us, length us, event | category | flops | bytes accessed | tf_op | source)
XLA Modules:
  0.0 267.6 jit_solution(15354226198498052951)
XLA Ops:
  5.0 13.2 %all-to-all-start = ((bf16[64,56,128]{2,1,0:T(8,128)(2,1)}), bf16[64,56,128]{2,1,0:T(8,128)(2,1)S(1)}, u32[]{:S(2)}, u32[]{:S(2)}) async-start(bf16[64,56,128]{2,1,0:T(8,128)(2,1)} %bitcast.8), calls=%async_computation | async-start | bytes 1835008 | tf_op jit(solution)/shard_map/all_to_all | solution.py:21
  19.1 1.8 reshape.66
  20.9 22.7 %all-to-all-done = bf16[64,56,128]{2,1,0:T(8,128)(2,1)S(1)} async-done(((bf16[64,56,128]{2,1,0:T(8,128)(2,1)}), bf16[64,56,128]{2,1,0:T(8,128)(2,1)S(1)}, u32[]{:S(2)}, u32[]{:S(2)}) %all-to-all-start) | async-done | bytes 917536 | tf_op jit(solution)/shard_map/all_to_all | solution.py:21
  43.5 7.0 %all-to-all-start.1 = ((bf16[64,112,128]{2,1,0:T(8,128)(2,1)}), bf16[64,112,128]{2,1,0:T(8,128)(2,1)}, u32[]{:S(2)}, u32[]{:S(2)}) async-start(bf16[64,112,128]{2,1,0:T(8,128)(2,1)} %reshape.66), calls=%async_computation.1 | async-start | bytes 3670016 | tf_op jit(solution)/shard_map/all_to_all | solution.py:21
  53.4 20.0 %collective-permute-done.1.refs_3_.refs_8_ = bf16[64,7168]{1,0:T(8,128)(2,1)S(1)} collective-permute-done((bf16[64,7168]{1,0:T(8,128)(2,1)S(1)}, bf16[64,7168]{1,0:T(8,128)(2,1)S(1)}, u32[]{:S(2)}, u32[]{:S(2)}) %collective-permute-start.1) | collective-permute-done | bytes 917536 | tf_op jit(solution)/shard_map/ppermute | solution.py:17
  75.2 1.9 collective-permute-start.2
  77.1 8.5 %collective-permute-done.3.refs_1_.refs_6_ = bf16[32,7168]{1,0:T(8,128)(2,1)S(1)} collective-permute-done((bf16[32,7168]{1,0:T(8,128)(2,1)S(1)}, bf16[32,7168]{1,0:T(8,128)(2,1)S(1)}, u32[]{:S(2)}, u32[]{:S(2)}) %collective-permute-start.3) | collective-permute-done | bytes 458784 | tf_op jit(solution)/shard_map/ppermute | solution.py:17
  86.1 10.4 %all-to-all-done.1 = bf16[64,112,128]{2,1,0:T(8,128)(2,1)} async-done(((bf16[64,112,128]{2,1,0:T(8,128)(2,1)}), bf16[64,112,128]{2,1,0:T(8,128)(2,1)}, u32[]{:S(2)}, u32[]{:S(2)}) %all-to-all-start.1) | async-done | bytes 1835040 | tf_op jit(solution)/shard_map/all_to_all | solution.py:21
  96.5 2.7 %reshape.69.refs_2_.refs_5_ = bf16[128,7168]{1,0:T(8,128)(2,1)S(1)} reshape(bf16[64,112,128]{2,1,0:T(8,128)(2,1)} %all-to-all-done.1) | data formatting | bytes 3670016 | tf_op jit(solution)/shard_map/reshape | solution.py:148
  102.0 8.5 %shard_map.110 = (bf16[256,256]{1,0:T(8,128)(2,1)}, bf16[256,256]{1,0:T(8,128)(2,1)}, bf16[256,256]{1,0:T(8,128)(2,1)}, bf16[32,3712]{1,0:T(8,128)(2,1)}, bf16[3...) custom-call(bf16[32,7168]{1,0:T(8,128)(2,1)} %collective-permute-don, ...), custom_call_target="tpu_custom_call" | custom-call | flops 1000000 | bytes 1000000 | tf_op jit(solution)/shard_map/pallas_call | solution.py:94
  110.7 2.7 collective-permute-start.9
  113.3 29.2 %collective-permute-done.5.refs_1_.refs_4_ = bf16[128,7168]{1,0:T(8,128)(2,1)} collective-permute-done((bf16[128,7168]{1,0:T(8,128)(2,1)S(1)}, bf16[128,7168]{1,0:T(8,128)(2,1)}, u32[]{:S(2)}, u32[]{:S(2)}) %collective-permute-start.5) | collective-permute-done | bytes 1835040 | tf_op jit(solution)/shard_map/ppermute | solution.py:17
  143.9 2.3 slice.99
  149.9 2.7 collective-permute-start.11
  152.6 9.9 %shard_map.111 = (bf16[384,256]{1,0:T(8,128)(2,1)}, bf16[384,256]{1,0:T(8,128)(2,1)}, bf16[384,256]{1,0:T(8,128)(2,1)}, bf16[64,3712]{1,0:T(8,128)(2,1)}, bf16[6...) custom-call(bf16[128,7168]{1,0:T(8,128)(2,1)} %collective-permute-done.4.re, ...), custom_call_target="tpu_custom_call" | custom-call | flops 1000000 | bytes 1000000 | tf_op jit(solution)/shard_map/pallas_call | solution.py:94
  162.5 17.4 %collective-permute-done.10 = bf16[64,3712]{1,0:T(8,128)(2,1)} collective-permute-done((bf16[64,3712]{1,0:T(8,128)(2,1)S(1)}, bf16[64,3712]{1,0:T(8,128)(2,1)}, u32[]{:S(2)}, u32[]{:S(2)}) %collective-permute-start.10) | collective-permute-done | bytes 475168 | tf_op jit(solution)/shard_map/ppermute | solution.py:17
  180.4 2.3 collective-permute-start.15
  182.7 7.4 %shard_map.112 = (bf16[128,256]{1,0:T(8,128)(2,1)}, bf16[128,256]{1,0:T(8,128)(2,1)}, bf16[128,256]{1,0:T(8,128)(2,1)}, bf16[64,3712]{1,0:T(8,128)(2,1)}, bf16[64,3712]{1,0:T(8,128)(2,1)}) custom-call(bf16[64,7168]{1,0:T(8,128)(2,1)} %copy-done.13, bf16[64,7168]{1,0:T(8,128)(2,1)} %copy-done.11, bf16[64,7168]{1,0:T(8,128)(2,1)} %copy-done.13, ...), custom_call_target="tpu_custom_call" | custom-call | flops 1000000 | bytes 1000000 | tf_op jit(solution)/shard_map/pallas_call | solution.py:94
  190.1 2.7 collective-permute-start.16
  195.3 6.8 %all-to-all-start.2 = ((bf16[64,29,128]{2,1,0:T(8,128)(2,1)}), bf16[64,29,128]{2,1,0:T(8,128)(2,1)S(1)}, u32[]{:S(2)}, u32[]{:S(2)}) async-start(bf16[64,29,128]{2,1,0:T(8,128)(2,1)} %reshape.70), calls=%async_computation.2 | async-start | bytes 1048576 | tf_op jit(solution)/shard_map/all_to_all | solution.py:21
  204.7 2.5 fusion.57
  207.7 2.7 %collective-permute-start.17 = (bf16[64,3712]{1,0:T(8,128)(2,1)S(1)}, bf16[64,3712]{1,0:T(8,128)(2,1)S(1)}, u32[]{:S(2)}, u32[]{:S(2)}) collective-permute-start(bf16[64,3712]{1,0:T(8,128)(2,1)S(1)} %add_convert_fusion.2), channel_id=1, source_target_pairs={{0,192},{64,0},{128,64},{192,128},{1,193},{65,1},{129,65},{193,129... | collective-permute-start | bytes 1425416 | tf_op jit(solution)/shard_map/ppermute | solution.py:17
  210.4 2.5 fusion.56
  212.9 2.6 fusion.58
  215.5 5.2 %collective-permute-done.13 = bf16[64,3712]{1,0:T(8,128)(2,1)S(1)} collective-permute-done((bf16[64,3712]{1,0:T(8,128)(2,1)S(1)}, bf16[64,3712]{1,0:T(8,128)(2,1)S(1)}, u32[]{:S(2)}, u32[]{:S(2)}) %collective-permute-start.13) | collective-permute-done | bytes 475168 | tf_op jit(solution)/shard_map/ppermute | solution.py:17
  222.4 2.2 reshape.72
  224.6 11.2 %all-to-all-start.3 = ((bf16[64,58,128]{2,1,0:T(8,128)(2,1)}), bf16[64,58,128]{2,1,0:T(8,128)(2,1)S(1)}, u32[]{:S(2)}, u32[]{:S(2)}) async-start(bf16[64,58,128]{2,1,0:T(8,128)(2,1)} %reshape.72), calls=%async_computation.3 | async-start | bytes 2097152 | tf_op jit(solution)/shard_map/all_to_all | solution.py:21
  240.1 1.9 copy-done.4
  243.6 1.9 fusion.3
  247.7 1.9 fusion.5
  251.9 1.9 fusion.4
  253.8 10.2 %all-to-all-done.3 = bf16[64,58,128]{2,1,0:T(8,128)(2,1)S(1)} async-done(((bf16[64,58,128]{2,1,0:T(8,128)(2,1)}), bf16[64,58,128]{2,1,0:T(8,128)(2,1)S(1)}, u32[]{:S(2)}, u32[]{:S(2)}) %all-to-all-start.3) | async-done | bytes 950304 | tf_op jit(solution)/shard_map/all_to_all | solution.py:21
  (151 shorter events, 39.7 us)
Async XLA Ops:
  5.0 38.5 %all-to-all-start = ((bf16[64,56,128]{2,1,0:T(8,128)(2,1)}), bf16[64,56,128]{2,1,0:T(8,128)(2,1)S(1)}, u32[]{:S(2)}, u32[]{:S(2)}) async-start(bf16[64,56,128]{2,1,0:T(8,128)(2,1)} %bitcast.8), calls=%async_computation | async-start | bytes 1835008 | tf_op jit(solution)/shard_map/all_to_all | solution.py:21
  43.5 53.0 %all-to-all-start.1 = ((bf16[64,112,128]{2,1,0:T(8,128)(2,1)}), bf16[64,112,128]{2,1,0:T(8,128)(2,1)}, u32[]{:S(2)}, u32[]{:S(2)}) async-start(bf16[64,112,128]{2,1,0:T(8,128)(2,1)} %reshape.66), calls=%async_computation.1 | async-start | bytes 3670016 | tf_op jit(solution)/shard_map/all_to_all | solution.py:21
  50.6 48.6 %copy-start.2 = (bf16[8,8,56,128]{3,1,2,0:T(8,128)(2,1)}, bf16[8,8,56,128]{3,1,2,0:T(8,128)(2,1)S(1)}, u32[]{:S(2)}) copy-start(bf16[8,8,56,128]{3,1,2,0:T(8,128)(2,1)S(1)} %copy.39) | copy-start | bytes 2752516
  50.6 22.8 %collective-permute-start.1 = (bf16[64,7168]{1,0:T(8,128)(2,1)S(1)}, bf16[64,7168]{1,0:T(8,128)(2,1)S(1)}, u32[]{:S(2)}, u32[]{:S(2)}) collective-permute-start(bf16[64,7168]{1,0:T(8,128)(2,1)S(1)} %bitcast.48), channel_id=1, source_target_pairs={{0,64},{64,128},{128,192},{192,0},{1,65},{65,129},{129,193},{193,1... | collective-permute-start | bytes 2752520 | tf_op jit(solution)/shard_map/ppermute | solution.py:17
  51.9 21.6 %collective-permute-start = (bf16[64,7168]{1,0:T(8,128)(2,1)S(1)}, bf16[64,7168]{1,0:T(8,128)(2,1)S(1)}, u32[]{:S(2)}, u32[]{:S(2)}) collective-permute-start(bf16[64,7168]{1,0:T(8,128)(2,1)S(1)} %bitcast.49), channel_id=1, source_target_pairs={{0,192},{64,0},{128,64},{192,128},{1,193},{65,1},{129,65},{193,129... | collective-permute-start | bytes 2752520 | tf_op jit(solution)/shard_map/ppermute | solution.py:17
  73.4 12.1 %collective-permute-start.3 = (bf16[32,7168]{1,0:T(8,128)(2,1)S(1)}, bf16[32,7168]{1,0:T(8,128)(2,1)S(1)}, u32[]{:S(2)}, u32[]{:S(2)}) collective-permute-start(bf16[32,7168]{1,0:T(8,128)(2,1)S(1)} %slice.129), channel_id=1, source_target_pairs={{0,64},{64,128},{128,192},{192,0},{1,65},{65,129},{129,193},{193,1... | collective-permute-start | bytes 1376264 | tf_op jit(solution)/shard_map/ppermute | solution.py:17
  75.2 10.9 %collective-permute-start.2 = (bf16[32,7168]{1,0:T(8,128)(2,1)S(1)}, bf16[32,7168]{1,0:T(8,128)(2,1)}, u32[]{:S(2)}, u32[]{:S(2)}) collective-permute-start(bf16[32,7168]{1,0:T(8,128)(2,1)S(1)} %slice.128), channel_id=1, source_target_pairs={{0,192},{64,0},{128,64},{192,128},{1,193},{65,1},{129,65},{193,129... | collective-permute-start | bytes 1376264 | tf_op jit(solution)/shard_map/ppermute | solution.py:17
  85.6 16.4 %copy-start.15 = (bf16[32,7168]{1,0:T(8,128)(2,1)}, bf16[32,7168]{1,0:T(8,128)(2,1)S(1)}, u32[]{:S(2)}) copy-start(bf16[32,7168]{1,0:T(8,128)(2,1)S(1)} %collective-permute-done.3.refs_1_.refs_6_) | copy-start | bytes 1376260
  99.3 11.3 %copy-start = (bf16[128,7168]{1,0:T(8,128)(2,1)}, bf16[128,7168]{1,0:T(8,128)(2,1)S(1)}, u32[]{:S(2)}) copy-start(bf16[128,7168]{1,0:T(8,128)(2,1)S(1)} %reshape.69.refs_2_.refs_5_) | copy-start | bytes 5505028
  99.3 43.3 %collective-permute-start.5 = (bf16[128,7168]{1,0:T(8,128)(2,1)S(1)}, bf16[128,7168]{1,0:T(8,128)(2,1)}, u32[]{:S(2)}, u32[]{:S(2)}) collective-permute-start(bf16[128,7168]{1,0:T(8,128)(2,1)S(1)} %reshape.69.refs_2_.refs_5_), channel_id=1, source_target_pairs={{0,64},{64,128},{128,192},{192,0},{1,65},{65,129},{129,193},{193,1... | collective-permute-start | bytes 5505032 | tf_op jit(solution)/shard_map/ppermute | solution.py:17
  100.6 42.0 %collective-permute-start.4 = (bf16[128,7168]{1,0:T(8,128)(2,1)S(1)}, bf16[128,7168]{1,0:T(8,128)(2,1)}, u32[]{:S(2)}, u32[]{:S(2)}) collective-permute-start(bf16[128,7168]{1,0:T(8,128)(2,1)S(1)} %reshape.69.refs_2_.refs_5_), channel_id=1, source_target_pairs={{0,192},{64,0},{128,64},{192,128},{1,193},{65,1},{129,65},{193,129... | collective-permute-start | bytes 5505032 | tf_op jit(solution)/shard_map/ppermute | solution.py:17
  110.6 38.3 %copy-start.22 = (bf16[32,3712]{1,0:T(8,128)(2,1)S(1)}, bf16[32,3712]{1,0:T(8,128)(2,1)}, u32[]{:S(2)}) copy-start(bf16[32,3712]{1,0:T(8,128)(2,1)} %get-tuple-element.99) | copy-start | bytes 712708
  110.6 38.3 %collective-permute-start.8 = (bf16[32,3712]{1,0:T(8,128)(2,1)}, bf16[32,3712]{1,0:T(8,128)(2,1)S(1)}, u32[]{:S(2)}, u32[]{:S(2)}) collective-permute-start(bf16[32,3712]{1,0:T(8,128)(2,1)} %get-tuple-element.100), channel_id=1, source_target_pairs={{0,64},{64,128},{128,192},{192,0},{1,65},{65,129},{129,193},{193,1... | collective-permute-start | bytes 712712 | tf_op jit(solution)/shard_map/ppermute | solution.py:17
  110.7 38.3 %collective-permute-start.9 = (bf16[32,3712]{1,0:T(8,128)(2,1)}, bf16[32,3712]{1,0:T(8,128)(2,1)S(1)}, u32[]{:S(2)}, u32[]{:S(2)}) collective-permute-start(bf16[32,3712]{1,0:T(8,128)(2,1)} %get-tuple-element.104), channel_id=1, source_target_pairs={{0,192},{64,0},{128,64},{192,128},{1,193},{65,1},{129,65},{193,129... | collective-permute-start | bytes 712712 | tf_op jit(solution)/shard_map/ppermute | solution.py:17
  142.6 6.3 %copy-start.24 = (bf16[32,3712]{1,0:T(8,128)(2,1)S(1)}, bf16[32,3712]{1,0:T(8,128)(2,1)}, u32[]{:S(2)}) copy-start(bf16[32,3712]{1,0:T(8,128)(2,1)} %get-tuple-element.101) | copy-start | bytes 712708
  146.1 6.4 %copy-start.32 = (bf16[16,8]{0,1:T(8,128)(2,1)S(1)}, bf16[16,8]{0,1:T(8,128)(2,1)}, u32[]{:S(2)}) copy-start(bf16[16,8]{0,1:T(8,128)(2,1)} %param.10) | copy-start | bytes 772
  146.1 33.8 %collective-permute-start.7 = (bf16[64,7168]{1,0:T(8,128)(2,1)}, bf16[64,7168]{1,0:T(8,128)(2,1)S(1)}, u32[]{:S(2)}, u32[]{:S(2)}) collective-permute-start(bf16[64,7168]{1,0:T(8,128)(2,1)} %slice.99), channel_id=1, source_target_pairs={{0,64},{64,128},{128,192},{192,0},{1,65},{65,129},{129,193},{193,1... | collective-permute-start | bytes 2752520 | tf_op jit(solution)/shard_map/ppermute | solution.py:17
  147.4 32.6 %collective-permute-start.6 = (bf16[64,7168]{1,0:T(8,128)(2,1)S(1)}, bf16[64,7168]{1,0:T(8,128)(2,1)S(1)}, u32[]{:S(2)}, u32[]{:S(2)}) collective-permute-start(bf16[64,7168]{1,0:T(8,128)(2,1)S(1)} %slice.98), channel_id=1, source_target_pairs={{0,192},{64,0},{128,64},{192,128},{1,193},{65,1},{129,65},{193,129... | collective-permute-start | bytes 2752520 | tf_op jit(solution)/shard_map/ppermute | solution.py:17
  149.9 30.0 %collective-permute-start.10 = (bf16[64,3712]{1,0:T(8,128)(2,1)S(1)}, bf16[64,3712]{1,0:T(8,128)(2,1)}, u32[]{:S(2)}, u32[]{:S(2)}) collective-permute-start(bf16[64,3712]{1,0:T(8,128)(2,1)S(1)} %pad_maximum_fusion.6), channel_id=1, source_target_pairs={{0,64},{64,128},{128,192},{192,0},{1,65},{65,129},{129,193},{193,1... | collective-permute-start | bytes 1425416 | tf_op jit(solution)/shard_map/ppermute | solution.py:17
  149.9 30.0 %collective-permute-start.11 = (bf16[64,3712]{1,0:T(8,128)(2,1)}, bf16[64,3712]{1,0:T(8,128)(2,1)}, u32[]{:S(2)}, u32[]{:S(2)}) collective-permute-start(bf16[64,3712]{1,0:T(8,128)(2,1)} %pad_maximum_fusion.7), channel_id=1, source_target_pairs={{0,192},{64,0},{128,64},{192,128},{1,193},{65,1},{129,65},{193,129... | collective-permute-start | bytes 1425416 | tf_op jit(solution)/shard_map/ppermute | solution.py:17
  180.0 12.8 %copy-start.20 = (bf16[64,3712]{1,0:T(8,128)(2,1)S(1)}, bf16[64,3712]{1,0:T(8,128)(2,1)}, u32[]{:S(2)}) copy-start(bf16[64,3712]{1,0:T(8,128)(2,1)} %get-tuple-element.125) | copy-start | bytes 1425412
  180.0 35.5 %collective-permute-start.14 = (bf16[64,3712]{1,0:T(8,128)(2,1)}, bf16[64,3712]{1,0:T(8,128)(2,1)S(1)}, u32[]{:S(2)}, u32[]{:S(2)}) collective-permute-start(bf16[64,3712]{1,0:T(8,128)(2,1)} %get-tuple-element.121), channel_id=1, source_target_pairs={{0,64},{64,128},{128,192},{192,0},{1,65},{65,129},{129,193},{193,1... | collective-permute-start | bytes 1425416 | tf_op jit(solution)/shard_map/ppermute | solution.py:17
  180.4 35.1 %collective-permute-start.15 = (bf16[64,3712]{1,0:T(8,128)(2,1)}, bf16[64,3712]{1,0:T(8,128)(2,1)}, u32[]{:S(2)}, u32[]{:S(2)}) collective-permute-start(bf16[64,3712]{1,0:T(8,128)(2,1)} %get-tuple-element.122), channel_id=1, source_target_pairs={{0,192},{64,0},{128,64},{192,128},{1,193},{65,1},{129,65},{193,129... | collective-permute-start | bytes 1425416 | tf_op jit(solution)/shard_map/ppermute | solution.py:17
  190.1 17.0 %collective-permute-start.12 = (bf16[64,3712]{1,0:T(8,128)(2,1)}, bf16[64,3712]{1,0:T(8,128)(2,1)S(1)}, u32[]{:S(2)}, u32[]{:S(2)}) collective-permute-start(bf16[64,3712]{1,0:T(8,128)(2,1)} %get-tuple-element.120), channel_id=1, source_target_pairs={{0,64},{64,128},{128,192},{192,0},{1,65},{65,129},{129,193},{193,1... | collective-permute-start | bytes 1425416 | tf_op jit(solution)/shard_map/ppermute | solution.py:17
  190.1 17.4 %collective-permute-start.16 = (bf16[64,3712]{1,0:T(8,128)(2,1)}, bf16[64,3712]{1,0:T(8,128)(2,1)S(1)}, u32[]{:S(2)}, u32[]{:S(2)}) collective-permute-start(bf16[64,3712]{1,0:T(8,128)(2,1)} %get-tuple-element.124), channel_id=1, source_target_pairs={{0,192},{64,0},{128,64},{192,128},{1,193},{65,1},{129,65},{193,129... | collective-permute-start | bytes 1425416 | tf_op jit(solution)/shard_map/ppermute | solution.py:17
  194.1 9.1 %copy-start.16 = (bf16[32,7168]{1,0:T(8,128)(2,1)S(1)}, bf16[32,7168]{1,0:T(8,128)(2,1)}, u32[]{:S(2)}) copy-start(bf16[32,7168]{1,0:T(8,128)(2,1)} %copy-done.15) | copy-start | bytes 1376260
  194.2 9.2 %copy-start.8 = (bf16[64,7168]{1,0:T(8,128)(2,1)S(1)}, bf16[64,7168]{1,0:T(8,128)(2,1)}, u32[]{:S(2)}) copy-start(bf16[64,7168]{1,0:T(8,128)(2,1)} %copy-done.7) | copy-start | bytes 2752516
  195.3 26.9 %all-to-all-start.2 = ((bf16[64,29,128]{2,1,0:T(8,128)(2,1)}), bf16[64,29,128]{2,1,0:T(8,128)(2,1)S(1)}, u32[]{:S(2)}, u32[]{:S(2)}) async-start(bf16[64,29,128]{2,1,0:T(8,128)(2,1)} %reshape.70), calls=%async_computation.2 | async-start | bytes 1048576 | tf_op jit(solution)/shard_map/all_to_all | solution.py:21
  207.3 13.5 %collective-permute-start.13 = (bf16[64,3712]{1,0:T(8,128)(2,1)S(1)}, bf16[64,3712]{1,0:T(8,128)(2,1)S(1)}, u32[]{:S(2)}, u32[]{:S(2)}) collective-permute-start(bf16[64,3712]{1,0:T(8,128)(2,1)S(1)} %add_convert_fusion.3), channel_id=1, source_target_pairs={{0,64},{64,128},{128,192},{192,0},{1,65},{65,129},{129,193},{193,1... | collective-permute-start | bytes 1425416 | tf_op jit(solution)/shard_map/ppermute | solution.py:17
  207.7 13.0 %collective-permute-start.17 = (bf16[64,3712]{1,0:T(8,128)(2,1)S(1)}, bf16[64,3712]{1,0:T(8,128)(2,1)S(1)}, u32[]{:S(2)}, u32[]{:S(2)}) collective-permute-start(bf16[64,3712]{1,0:T(8,128)(2,1)S(1)} %add_convert_fusion.2), channel_id=1, source_target_pairs={{0,192},{64,0},{128,64},{192,128},{1,193},{65,1},{129,65},{193,129... | collective-permute-start | bytes 1425416 | tf_op jit(solution)/shard_map/ppermute | solution.py:17
  212.9 7.8 %copy-start.17 = (bf16[128,3712]{1,0:T(8,128)(2,1)S(1)}, bf16[128,3712]{1,0:T(8,128)(2,1)}, u32[]{:S(2)}) copy-start(bf16[128,3712]{1,0:T(8,128)(2,1)} %get-tuple-element.116) | copy-start | bytes 2850820
  224.6 39.3 %all-to-all-start.3 = ((bf16[64,58,128]{2,1,0:T(8,128)(2,1)}), bf16[64,58,128]{2,1,0:T(8,128)(2,1)S(1)}, u32[]{:S(2)}, u32[]{:S(2)}) async-start(bf16[64,58,128]{2,1,0:T(8,128)(2,1)} %reshape.72), calls=%async_computation.3 | async-start | bytes 2097152 | tf_op jit(solution)/shard_map/all_to_all | solution.py:21
  (25 other events, 60.6 us)

commit v2 on v1

--- a/solution.py
+++ b/solution.py
@@ -194,7 +194,7 @@
     came0 = shift(up0, 1), shift(down0, -1)
     size = own1.shape[0] // 2
     near1, parts1 = forward(one1 + (own1,), [size] * 4 + [2 * size])
-    two1, came0, parts1 = bar((two1, came0, parts1))
+    two1, parts1 = bar((two1, parts1))
     up_top, up_low, down_top, down_low, mine = parts1
     early = shift(up_low, 1), shift(down_top, -1)
     far1, far = forward(two1, [size] * 2)

time: 269 us -> 261 us (0.970)
  waiting for transfers between devices: 124 us -> 115 us
    ppermute x18, waiting for transfers between devices: 80.9 us -> 71.3 us  [shift(): lax.ppermute(value, 'dp', [(i, (i + step) % size) for i in range(size)])]
  transfers between devices with their start and end apart: 22 -> 22, of which waited for: 10 -> 12; matrix products, arithmetic and copies ran while one was open for 13% -> 13% of each run, Pallas kernels for 10% -> 10%
where the time goes in v2:
time: 261 us; the launch traced here: 260 us
  waiting for transfers between devices  115 us (44%)
  starting transfers between devices  64 us (25%)
  local copies, waits for them, and re-layouts  29.2 us (11%)
  Pallas kernels  25.9 us (10%)
  matrix products  20.1 us (8%)
  other arithmetic  4.91 us (2%)
    ppermute x18, waiting for transfers between devices, shift(): lax.ppermute(value, 'dp', [(i, (i + step) % size) for i in range(size)])  71.3 us
    all_to_all x4, waiting for transfers between devices, swap(): lax.all_to_all(value, ('node', 'local'), split_axis=0, concat_axis=0, til...  43.3 us
    all_to_all x4, starting transfers between devices, swap(): lax.all_to_all(value, ('node', 'local'), split_axis=0, concat_axis=0, til...  40.1 us
    pallas_call x3, Pallas kernels, expert_rows(): pl.pallas_call(lambda *refs: expert_kernel(steps, len(blocks), *refs), gr...  25.9 us
    ppermute x18, starting transfers between devices, shift(): lax.ppermute(value, 'dp', [(i, (i + step) % size) for i in range(size)])  23.9 us
    dot_general x15, matrix products, dot(): lax.dot_general(a, b, (((ca,), (cb,)), ((), ())), preferred_element_type=...  20.1 us
    unnamed x80, local copies, waits for them, and re-layouts  11.9 us
  transfers between devices with their start and end apart: 22, of which 12 were waited for; matrix products, arithmetic and copies ran while one was open for 13% of the time, Pallas kernels for 10%

profile of v2, /device:TPU:1, one launch (start us, length us, event | category | flops | bytes accessed | tf_op | source)
XLA Modules:
  0.0 259.9 jit_solution(1451589212225692881)
XLA Ops:
  5.0 13.2 %all-to-all-start = ((bf16[64,56,128]{2,1,0:T(8,128)(2,1)}), bf16[64,56,128]{2,1,0:T(8,128)(2,1)S(1)}, u32[]{:S(2)}, u32[]{:S(2)}) async-start(bf16[64,56,128]{2,1,0:T(8,128)(2,1)} %bitcast.8), calls=%async_computation | async-start | bytes 1835008 | tf_op jit(solution)/shard_map/all_to_all | solution.py:21
  19.1 1.8 reshape.66
  20.9 22.7 %all-to-all-done = bf16[64,56,128]{2,1,0:T(8,128)(2,1)S(1)} async-done(((bf16[64,56,128]{2,1,0:T(8,128)(2,1)}), bf16[64,56,128]{2,1,0:T(8,128)(2,1)S(1)}, u32[]{:S(2)}, u32[]{:S(2)}) %all-to-all-start) | async-done | bytes 917536 | tf_op jit(solution)/shard_map/all_to_all | solution.py:21
  43.5 7.0 %all-to-all-start.1 = ((bf16[64,112,128]{2,1,0:T(8,128)(2,1)}), bf16[64,112,128]{2,1,0:T(8,128)(2,1)}, u32[]{:S(2)}, u32[]{:S(2)}) async-start(bf16[64,112,128]{2,1,0:T(8,128)(2,1)} %reshape.66), calls=%async_computation.1 | async-start | bytes 3670016 | tf_op jit(solution)/shard_map/all_to_all | solution.py:21
  53.4 20.0 %collective-permute-done.1.refs_3_.refs_8_ = bf16[64,7168]{1,0:T(8,128)(2,1)S(1)} collective-permute-done((bf16[64,7168]{1,0:T(8,128)(2,1)S(1)}, bf16[64,7168]{1,0:T(8,128)(2,1)S(1)}, u32[]{:S(2)}, u32[]{:S(2)}) %collective-permute-start.1) | collective-permute-done | bytes 917536 | tf_op jit(solution)/shard_map/ppermute | solution.py:17
  75.2 1.9 collective-permute-start.2
  77.1 8.5 %collective-permute-done.3.refs_1_.refs_6_ = bf16[32,7168]{1,0:T(8,128)(2,1)S(1)} collective-permute-done((bf16[32,7168]{1,0:T(8,128)(2,1)S(1)}, bf16[32,7168]{1,0:T(8,128)(2,1)S(1)}, u32[]{:S(2)}, u32[]{:S(2)}) %collective-permute-start.3) | collective-permute-done | bytes 458784 | tf_op jit(solution)/shard_map/ppermute | solution.py:17
  86.1 10.4 %all-to-all-done.1 = bf16[64,112,128]{2,1,0:T(8,128)(2,1)} async-done(((bf16[64,112,128]{2,1,0:T(8,128)(2,1)}), bf16[64,112,128]{2,1,0:T(8,128)(2,1)}, u32[]{:S(2)}, u32[]{:S(2)}) %all-to-all-start.1) | async-done | bytes 1835040 | tf_op jit(solution)/shard_map/all_to_all | solution.py:21
  96.5 2.7 %reshape.69.refs_2_.refs_5_ = bf16[128,7168]{1,0:T(8,128)(2,1)S(1)} reshape(bf16[64,112,128]{2,1,0:T(8,128)(2,1)} %all-to-all-done.1) | data formatting | bytes 3670016 | tf_op jit(solution)/shard_map/reshape | solution.py:148
  102.0 8.5 %shard_map.110 = (bf16[256,256]{1,0:T(8,128)(2,1)}, bf16[256,256]{1,0:T(8,128)(2,1)}, bf16[256,256]{1,0:T(8,128)(2,1)}, bf16[32,3712]{1,0:T(8,128)(2,1)}, bf16[3...) custom-call(bf16[32,7168]{1,0:T(8,128)(2,1)} %collective-permute-don, ...), custom_call_target="tpu_custom_call" | custom-call | flops 1000000 | bytes 1000000 | tf_op jit(solution)/shard_map/pallas_call | solution.py:94
  110.7 2.7 %collective-permute-start.9 = (bf16[32,3712]{1,0:T(8,128)(2,1)}, bf16[32,3712]{1,0:T(8,128)(2,1)S(1)}, u32[]{:S(2)}, u32[]{:S(2)}) collective-permute-start(bf16[32,3712]{1,0:T(8,128)(2,1)} %get-tuple-element.102), channel_id=1, source_target_pairs={{0,192},{64,0},{128,64},{192,128},{1,193},{65,1},{129,65},{193,129... | collective-permute-start | bytes 712712 | tf_op jit(solution)/shard_map/ppermute | solution.py:17
  113.3 29.2 %collective-permute-done.5.refs_1_.refs_4_ = bf16[128,7168]{1,0:T(8,128)(2,1)} collective-permute-done((bf16[128,7168]{1,0:T(8,128)(2,1)S(1)}, bf16[128,7168]{1,0:T(8,128)(2,1)}, u32[]{:S(2)}, u32[]{:S(2)}) %collective-permute-start.5) | collective-permute-done | bytes 1835040 | tf_op jit(solution)/shard_map/ppermute | solution.py:17
  143.9 2.3 slice.99
  149.9 2.7 %collective-permute-start.17 = (bf16[64,3712]{1,0:T(8,128)(2,1)}, bf16[64,3712]{1,0:T(8,128)(2,1)}, u32[]{:S(2)}, u32[]{:S(2)}) collective-permute-start(bf16[64,3712]{1,0:T(8,128)(2,1)} %pad_maximum_fusion.7), channel_id=1, source_target_pairs={{0,192},{64,0},{128,64},{192,128},{1,193},{65,1},{129,65},{193,129... | collective-permute-start | bytes 1425416 | tf_op jit(solution)/shard_map/ppermute | solution.py:17
  152.6 9.9 %shard_map.111 = (bf16[384,256]{1,0:T(8,128)(2,1)}, bf16[384,256]{1,0:T(8,128)(2,1)}, bf16[384,256]{1,0:T(8,128)(2,1)}, bf16[64,3712]{1,0:T(8,128)(2,1)}, bf16[6...) custom-call(bf16[128,7168]{1,0:T(8,128)(2,1)} %collective-permute-done.4.re, ...), custom_call_target="tpu_custom_call" | custom-call | flops 1000000 | bytes 1000000 | tf_op jit(solution)/shard_map/pallas_call | solution.py:94
  162.5 7.1 %collective-permute-done.7.refs_1_.refs_3_ = bf16[64,7168]{1,0:T(8,128)(2,1)S(1)} collective-permute-done((bf16[64,7168]{1,0:T(8,128)(2,1)}, bf16[64,7168]{1,0:T(8,128)(2,1)S(1)}, u32[]{:S(2)}, u32[]{:S(2)}) %collective-permute-start.7) | collective-permute-done | bytes 917536 | tf_op jit(solution)/shard_map/ppermute | solution.py:17
  170.0 2.4 collective-permute-start.13
  172.4 7.4 %shard_map.112 = (bf16[128,256]{1,0:T(8,128)(2,1)}, bf16[128,256]{1,0:T(8,128)(2,1)}, bf16[128,256]{1,0:T(8,128)(2,1)}, bf16[64,3712]{1,0:T(8,128)(2,1)}, bf16[64,3712]{1,0:T(8,128)(2,1)}) custom-call(bf16[64,7168]{1,0:T(8,128)(2,1)} %copy-done.13, bf16[64,7168]{1,0:T(8,128)(2,1)} %copy-done.11, bf16[64,7168]{1,0:T(8,128)(2,1)} %copy-done.13, ...), custom_call_target="tpu_custom_call" | custom-call | flops 1000000 | bytes 1000000 | tf_op jit(solution)/shard_map/pallas_call | solution.py:94
  179.9 2.6 collective-permute-start.14
  185.0 9.3 %all-to-all-start.2 = ((bf16[64,29,128]{2,1,0:T(8,128)(2,1)}), bf16[64,29,128]{2,1,0:T(8,128)(2,1)S(1)}, u32[]{:S(2)}, u32[]{:S(2)}) async-start(bf16[64,29,128]{2,1,0:T(8,128)(2,1)} %reshape.70), calls=%async_computation.2 | async-start | bytes 1048576 | tf_op jit(solution)/shard_map/all_to_all | solution.py:21
  196.8 2.5 fusion.57
  200.8 2.7 %collective-permute-start.15 = (bf16[64,3712]{1,0:T(8,128)(2,1)S(1)}, bf16[64,3712]{1,0:T(8,128)(2,1)S(1)}, u32[]{:S(2)}, u32[]{:S(2)}) collective-permute-start(bf16[64,3712]{1,0:T(8,128)(2,1)S(1)} %add_convert_fusion.2), channel_id=1, source_target_pairs={{0,192},{64,0},{128,64},{192,128},{1,193},{65,1},{129,65},{193,129... | collective-permute-start | bytes 1425416 | tf_op jit(solution)/shard_map/ppermute | solution.py:17
  203.5 2.5 fusion.56
  206.0 2.6 fusion.58
  208.5 5.0 %collective-permute-done.11 = bf16[64,3712]{1,0:T(8,128)(2,1)S(1)} collective-permute-done((bf16[64,3712]{1,0:T(8,128)(2,1)S(1)}, bf16[64,3712]{1,0:T(8,128)(2,1)S(1)}, u32[]{:S(2)}, u32[]{:S(2)}) %collective-permute-start.11) | collective-permute-done | bytes 475168 | tf_op jit(solution)/shard_map/ppermute | solution.py:17
  215.3 2.2 reshape.72
  217.5 10.7 %all-to-all-start.3 = ((bf16[64,58,128]{2,1,0:T(8,128)(2,1)}), bf16[64,58,128]{2,1,0:T(8,128)(2,1)S(1)}, u32[]{:S(2)}, u32[]{:S(2)}) async-start(bf16[64,58,128]{2,1,0:T(8,128)(2,1)} %reshape.72), calls=%async_computation.3 | async-start | bytes 2097152 | tf_op jit(solution)/shard_map/all_to_all | solution.py:21
  232.5 1.9 copy-done.4
  235.9 1.9 fusion.3
  240.1 1.9 fusion.5
  244.2 1.9 fusion.4
  246.1 10.2 %all-to-all-done.3 = bf16[64,58,128]{2,1,0:T(8,128)(2,1)S(1)} async-done(((bf16[64,58,128]{2,1,0:T(8,128)(2,1)}), bf16[64,58,128]{2,1,0:T(8,128)(2,1)S(1)}, u32[]{:S(2)}, u32[]{:S(2)}) %all-to-all-start.3) | async-done | bytes 950304 | tf_op jit(solution)/shard_map/all_to_all | solution.py:21
  (151 shorter events, 40.7 us)
Async XLA Ops:
  5.0 38.5 %all-to-all-start = ((bf16[64,56,128]{2,1,0:T(8,128)(2,1)}), bf16[64,56,128]{2,1,0:T(8,128)(2,1)S(1)}, u32[]{:S(2)}, u32[]{:S(2)}) async-start(bf16[64,56,128]{2,1,0:T(8,128)(2,1)} %bitcast.8), calls=%async_computation | async-start | bytes 1835008 | tf_op jit(solution)/shard_map/all_to_all | solution.py:21
  43.5 53.0 %all-to-all-start.1 = ((bf16[64,112,128]{2,1,0:T(8,128)(2,1)}), bf16[64,112,128]{2,1,0:T(8,128)(2,1)}, u32[]{:S(2)}, u32[]{:S(2)}) async-start(bf16[64,112,128]{2,1,0:T(8,128)(2,1)} %reshape.66), calls=%async_computation.1 | async-start | bytes 3670016 | tf_op jit(solution)/shard_map/all_to_all | solution.py:21
  50.6 48.6 %copy-start.2 = (bf16[8,8,56,128]{3,1,2,0:T(8,128)(2,1)}, bf16[8,8,56,128]{3,1,2,0:T(8,128)(2,1)S(1)}, u32[]{:S(2)}) copy-start(bf16[8,8,56,128]{3,1,2,0:T(8,128)(2,1)S(1)} %copy.39) | copy-start | bytes 2752516
  50.6 22.8 %collective-permute-start.1 = (bf16[64,7168]{1,0:T(8,128)(2,1)S(1)}, bf16[64,7168]{1,0:T(8,128)(2,1)S(1)}, u32[]{:S(2)}, u32[]{:S(2)}) collective-permute-start(bf16[64,7168]{1,0:T(8,128)(2,1)S(1)} %bitcast.48), channel_id=1, source_target_pairs={{0,64},{64,128},{128,192},{192,0},{1,65},{65,129},{129,193},{193,1... | collective-permute-start | bytes 2752520 | tf_op jit(solution)/shard_map/ppermute | solution.py:17
  51.9 21.6 %collective-permute-start = (bf16[64,7168]{1,0:T(8,128)(2,1)S(1)}, bf16[64,7168]{1,0:T(8,128)(2,1)S(1)}, u32[]{:S(2)}, u32[]{:S(2)}) collective-permute-start(bf16[64,7168]{1,0:T(8,128)(2,1)S(1)} %bitcast.49), channel_id=1, source_target_pairs={{0,192},{64,0},{128,64},{192,128},{1,193},{65,1},{129,65},{193,129... | collective-permute-start | bytes 2752520 | tf_op jit(solution)/shard_map/ppermute | solution.py:17
  73.4 12.1 %collective-permute-start.3 = (bf16[32,7168]{1,0:T(8,128)(2,1)S(1)}, bf16[32,7168]{1,0:T(8,128)(2,1)S(1)}, u32[]{:S(2)}, u32[]{:S(2)}) collective-permute-start(bf16[32,7168]{1,0:T(8,128)(2,1)S(1)} %slice.129), channel_id=1, source_target_pairs={{0,64},{64,128},{128,192},{192,0},{1,65},{65,129},{129,193},{193,1... | collective-permute-start | bytes 1376264 | tf_op jit(solution)/shard_map/ppermute | solution.py:17
  75.2 10.9 %collective-permute-start.2 = (bf16[32,7168]{1,0:T(8,128)(2,1)S(1)}, bf16[32,7168]{1,0:T(8,128)(2,1)}, u32[]{:S(2)}, u32[]{:S(2)}) collective-permute-start(bf16[32,7168]{1,0:T(8,128)(2,1)S(1)} %slice.128), channel_id=1, source_target_pairs={{0,192},{64,0},{128,64},{192,128},{1,193},{65,1},{129,65},{193,129... | collective-permute-start | bytes 1376264 | tf_op jit(solution)/shard_map/ppermute | solution.py:17
  85.6 16.4 %copy-start.15 = (bf16[32,7168]{1,0:T(8,128)(2,1)}, bf16[32,7168]{1,0:T(8,128)(2,1)S(1)}, u32[]{:S(2)}) copy-start(bf16[32,7168]{1,0:T(8,128)(2,1)S(1)} %collective-permute-done.3.refs_1_.refs_6_) | copy-start | bytes 1376260
  99.3 11.3 %copy-start = (bf16[128,7168]{1,0:T(8,128)(2,1)}, bf16[128,7168]{1,0:T(8,128)(2,1)S(1)}, u32[]{:S(2)}) copy-start(bf16[128,7168]{1,0:T(8,128)(2,1)S(1)} %reshape.69.refs_2_.refs_5_) | copy-start | bytes 5505028
  99.3 43.3 %collective-permute-start.5 = (bf16[128,7168]{1,0:T(8,128)(2,1)S(1)}, bf16[128,7168]{1,0:T(8,128)(2,1)}, u32[]{:S(2)}, u32[]{:S(2)}) collective-permute-start(bf16[128,7168]{1,0:T(8,128)(2,1)S(1)} %reshape.69.refs_2_.refs_5_), channel_id=1, source_target_pairs={{0,64},{64,128},{128,192},{192,0},{1,65},{65,129},{129,193},{193,1... | collective-permute-start | bytes 5505032 | tf_op jit(solution)/shard_map/ppermute | solution.py:17
  100.6 42.0 %collective-permute-start.4 = (bf16[128,7168]{1,0:T(8,128)(2,1)S(1)}, bf16[128,7168]{1,0:T(8,128)(2,1)}, u32[]{:S(2)}, u32[]{:S(2)}) collective-permute-start(bf16[128,7168]{1,0:T(8,128)(2,1)S(1)} %reshape.69.refs_2_.refs_5_), channel_id=1, source_target_pairs={{0,192},{64,0},{128,64},{192,128},{1,193},{65,1},{129,65},{193,129... | collective-permute-start | bytes 5505032 | tf_op jit(solution)/shard_map/ppermute | solution.py:17
  110.6 38.3 %copy-start.22 = (bf16[32,3712]{1,0:T(8,128)(2,1)S(1)}, bf16[32,3712]{1,0:T(8,128)(2,1)}, u32[]{:S(2)}) copy-start(bf16[32,3712]{1,0:T(8,128)(2,1)} %get-tuple-element.97) | copy-start | bytes 712708
  110.6 38.3 %collective-permute-start.8 = (bf16[32,3712]{1,0:T(8,128)(2,1)}, bf16[32,3712]{1,0:T(8,128)(2,1)S(1)}, u32[]{:S(2)}, u32[]{:S(2)}) collective-permute-start(bf16[32,3712]{1,0:T(8,128)(2,1)} %get-tuple-element.98), channel_id=1, source_target_pairs={{0,64},{64,128},{128,192},{192,0},{1,65},{65,129},{129,193},{193,1... | collective-permute-start | bytes 712712 | tf_op jit(solution)/shard_map/ppermute | solution.py:17
  110.7 38.3 %collective-permute-start.9 = (bf16[32,3712]{1,0:T(8,128)(2,1)}, bf16[32,3712]{1,0:T(8,128)(2,1)S(1)}, u32[]{:S(2)}, u32[]{:S(2)}) collective-permute-start(bf16[32,3712]{1,0:T(8,128)(2,1)} %get-tuple-element.102), channel_id=1, source_target_pairs={{0,192},{64,0},{128,64},{192,128},{1,193},{65,1},{129,65},{193,129... | collective-permute-start | bytes 712712 | tf_op jit(solution)/shard_map/ppermute | solution.py:17
  142.6 6.3 %copy-start.24 = (bf16[32,3712]{1,0:T(8,128)(2,1)S(1)}, bf16[32,3712]{1,0:T(8,128)(2,1)}, u32[]{:S(2)}) copy-start(bf16[32,3712]{1,0:T(8,128)(2,1)} %get-tuple-element.99) | copy-start | bytes 712708
  146.1 6.4 %copy-start.32 = (bf16[16,8]{0,1:T(8,128)(2,1)S(1)}, bf16[16,8]{0,1:T(8,128)(2,1)}, u32[]{:S(2)}) copy-start(bf16[16,8]{0,1:T(8,128)(2,1)} %param.10) | copy-start | bytes 772
  146.1 23.5 %collective-permute-start.7 = (bf16[64,7168]{1,0:T(8,128)(2,1)}, bf16[64,7168]{1,0:T(8,128)(2,1)S(1)}, u32[]{:S(2)}, u32[]{:S(2)}) collective-permute-start(bf16[64,7168]{1,0:T(8,128)(2,1)} %slice.99), channel_id=1, source_target_pairs={{0,64},{64,128},{128,192},{192,0},{1,65},{65,129},{129,193},{193,1... | collective-permute-start | bytes 2752520 | tf_op jit(solution)/shard_map/ppermute | solution.py:17
  147.4 22.3 %collective-permute-start.6 = (bf16[64,7168]{1,0:T(8,128)(2,1)S(1)}, bf16[64,7168]{1,0:T(8,128)(2,1)S(1)}, u32[]{:S(2)}, u32[]{:S(2)}) collective-permute-start(bf16[64,7168]{1,0:T(8,128)(2,1)S(1)} %slice.98), channel_id=1, source_target_pairs={{0,192},{64,0},{128,64},{192,128},{1,193},{65,1},{129,65},{193,129... | collective-permute-start | bytes 2752520 | tf_op jit(solution)/shard_map/ppermute | solution.py:17
  149.9 30.1 %collective-permute-start.16 = (bf16[64,3712]{1,0:T(8,128)(2,1)S(1)}, bf16[64,3712]{1,0:T(8,128)(2,1)}, u32[]{:S(2)}, u32[]{:S(2)}) collective-permute-start(bf16[64,3712]{1,0:T(8,128)(2,1)S(1)} %pad_maximum_fusion.6), channel_id=1, source_target_pairs={{0,64},{64,128},{128,192},{192,0},{1,65},{65,129},{129,193},{193,1... | collective-permute-start | bytes 1425416 | tf_op jit(solution)/shard_map/ppermute | solution.py:17
  149.9 32.6 %collective-permute-start.17 = (bf16[64,3712]{1,0:T(8,128)(2,1)}, bf16[64,3712]{1,0:T(8,128)(2,1)}, u32[]{:S(2)}, u32[]{:S(2)}) collective-permute-start(bf16[64,3712]{1,0:T(8,128)(2,1)} %pad_maximum_fusion.7), channel_id=1, source_target_pairs={{0,192},{64,0},{128,64},{192,128},{1,193},{65,1},{129,65},{193,129... | collective-permute-start | bytes 1425416 | tf_op jit(solution)/shard_map/ppermute | solution.py:17
  169.6 12.9 %copy-start.20 = (bf16[64,3712]{1,0:T(8,128)(2,1)S(1)}, bf16[64,3712]{1,0:T(8,128)(2,1)}, u32[]{:S(2)}) copy-start(bf16[64,3712]{1,0:T(8,128)(2,1)} %get-tuple-element.121) | copy-start | bytes 1425412
  169.6 38.9 %collective-permute-start.12 = (bf16[64,3712]{1,0:T(8,128)(2,1)}, bf16[64,3712]{1,0:T(8,128)(2,1)}, u32[]{:S(2)}, u32[]{:S(2)}) collective-permute-start(bf16[64,3712]{1,0:T(8,128)(2,1)} %get-tuple-element.117), channel_id=1, source_target_pairs={{0,64},{64,128},{128,192},{192,0},{1,65},{65,129},{129,193},{193,1... | collective-permute-start | bytes 1425416 | tf_op jit(solution)/shard_map/ppermute | solution.py:17
  170.0 38.5 %collective-permute-start.13 = (bf16[64,3712]{1,0:T(8,128)(2,1)}, bf16[64,3712]{1,0:T(8,128)(2,1)}, u32[]{:S(2)}, u32[]{:S(2)}) collective-permute-start(bf16[64,3712]{1,0:T(8,128)(2,1)} %get-tuple-element.118), channel_id=1, source_target_pairs={{0,192},{64,0},{128,64},{192,128},{1,193},{65,1},{129,65},{193,129... | collective-permute-start | bytes 1425416 | tf_op jit(solution)/shard_map/ppermute | solution.py:17
  179.8 20.4 %collective-permute-start.10 = (bf16[64,3712]{1,0:T(8,128)(2,1)}, bf16[64,3712]{1,0:T(8,128)(2,1)S(1)}, u32[]{:S(2)}, u32[]{:S(2)}) collective-permute-start(bf16[64,3712]{1,0:T(8,128)(2,1)} %get-tuple-element.116), channel_id=1, source_target_pairs={{0,64},{64,128},{128,192},{192,0},{1,65},{65,129},{129,193},{193,1... | collective-permute-start | bytes 1425416 | tf_op jit(solution)/shard_map/ppermute | solution.py:17
  179.9 20.7 %collective-permute-start.14 = (bf16[64,3712]{1,0:T(8,128)(2,1)}, bf16[64,3712]{1,0:T(8,128)(2,1)S(1)}, u32[]{:S(2)}, u32[]{:S(2)}) collective-permute-start(bf16[64,3712]{1,0:T(8,128)(2,1)} %get-tuple-element.120), channel_id=1, source_target_pairs={{0,192},{64,0},{128,64},{192,128},{1,193},{65,1},{129,65},{193,129... | collective-permute-start | bytes 1425416 | tf_op jit(solution)/shard_map/ppermute | solution.py:17
  183.9 11.6 %copy-start.16 = (bf16[32,7168]{1,0:T(8,128)(2,1)S(1)}, bf16[32,7168]{1,0:T(8,128)(2,1)}, u32[]{:S(2)}) copy-start(bf16[32,7168]{1,0:T(8,128)(2,1)} %copy-done.15) | copy-start | bytes 1376260
  183.9 11.7 %copy-start.8 = (bf16[64,7168]{1,0:T(8,128)(2,1)S(1)}, bf16[64,7168]{1,0:T(8,128)(2,1)}, u32[]{:S(2)}) copy-start(bf16[64,7168]{1,0:T(8,128)(2,1)} %copy-done.7) | copy-start | bytes 2752516
  185.0 30.1 %all-to-all-start.2 = ((bf16[64,29,128]{2,1,0:T(8,128)(2,1)}), bf16[64,29,128]{2,1,0:T(8,128)(2,1)S(1)}, u32[]{:S(2)}, u32[]{:S(2)}) async-start(bf16[64,29,128]{2,1,0:T(8,128)(2,1)} %reshape.70), calls=%async_computation.2 | async-start | bytes 1048576 | tf_op jit(solution)/shard_map/all_to_all | solution.py:21
  200.3 13.2 %collective-permute-start.11 = (bf16[64,3712]{1,0:T(8,128)(2,1)S(1)}, bf16[64,3712]{1,0:T(8,128)(2,1)S(1)}, u32[]{:S(2)}, u32[]{:S(2)}) collective-permute-start(bf16[64,3712]{1,0:T(8,128)(2,1)S(1)} %add_convert_fusion.3), channel_id=1, source_target_pairs={{0,64},{64,128},{128,192},{192,0},{1,65},{65,129},{129,193},{193,1... | collective-permute-start | bytes 1425416 | tf_op jit(solution)/shard_map/ppermute | solution.py:17
  200.8 12.8 %collective-permute-start.15 = (bf16[64,3712]{1,0:T(8,128)(2,1)S(1)}, bf16[64,3712]{1,0:T(8,128)(2,1)S(1)}, u32[]{:S(2)}, u32[]{:S(2)}) collective-permute-start(bf16[64,3712]{1,0:T(8,128)(2,1)S(1)} %add_convert_fusion.2), channel_id=1, source_target_pairs={{0,192},{64,0},{128,64},{192,128},{1,193},{65,1},{129,65},{193,129... | collective-permute-start | bytes 1425416 | tf_op jit(solution)/shard_map/ppermute | solution.py:17
  206.0 7.5 %copy-start.17 = (bf16[128,3712]{1,0:T(8,128)(2,1)S(1)}, bf16[128,3712]{1,0:T(8,128)(2,1)}, u32[]{:S(2)}) copy-start(bf16[128,3712]{1,0:T(8,128)(2,1)} %get-tuple-element.112) | copy-start | bytes 2850820
  217.5 38.7 %all-to-all-start.3 = ((bf16[64,58,128]{2,1,0:T(8,128)(2,1)}), bf16[64,58,128]{2,1,0:T(8,128)(2,1)S(1)}, u32[]{:S(2)}, u32[]{:S(2)}) async-start(bf16[64,58,128]{2,1,0:T(8,128)(2,1)} %reshape.72), calls=%async_computation.3 | async-start | bytes 2097152 | tf_op jit(solution)/shard_map/all_to_all | solution.py:21
  (25 other events, 63.2 us)
